TPU v7x, 32 devices: a whole 2x2x4 slice. The times are simulated.
32 devices in a mesh: section: 4 (over z), node: 2 (over y), local: 4 (over x, core).
Axes of the slice: x: 2, y: 2, z: 4, core: 2. Of those that a mesh axis runs over, the one named last changes fastest.
Arguments:
- layer_input: bfloat16 [4, 320, 7168], P('section', 'node', 'local'), may hold values from -6 to 6
- out_grad: bfloat16 [4, 320, 7168], P('section', 'node', 'local'), may hold values from -1.796875 to 1.796875
- routes: int32 [4, 320, 1], P('section', 'node'), may hold values from 0 to 1; in each aligned block of 160 rows (0 to 159, 160 to 319, ..., all dimensions but the last counted through in order) at most 120 rows name the same one
- gates: bfloat16 [4, 320, 1], P('section', 'node'), may hold values from 0.049804688 to 1
- gate_weight: bfloat16 [4, 2, 7168, 1024], P('section', 'node', None, 'local'), may hold values from -0.0625 to 0.0625
- up_weight: bfloat16 [4, 2, 7168, 1024], P('section', 'node', None, 'local'), may hold values from -0.0625 to 0.0625
- down_weight: bfloat16 [4, 2, 1024, 7168], P('section', 'node', 'local'), may hold values from -0.1875 to 0.1875
Outputs:
- passed: bfloat16 [4, 320, 7168], P('section', 'node', 'local')
- gate_grad: float32 [4, 320, 1], P('section', 'node')
- gate_wgrad: bfloat16 [4, 2, 7168, 1024], P('section', 'node', None, 'local')
- up_wgrad: bfloat16 [4, 2, 7168, 1024], P('section', 'node', None, 'local')
- down_wgrad: bfloat16 [4, 2, 1024, 7168], P('section', 'node', 'local')
Inputs may be any that keep to these rules, and one draw needn't show every extreme that they name: Within each aligned block of 160 tokens of one layer (the tokens of one node), a token's 1 routes name different experts and no expert is named by more than 120 routes of the block; in every draw some block names some expert exactly 120 times.
All inputs are finite; a program needn't handle non-finite values.
Results may differ from a plain program's by a relative error of at most 0.0065.
Values may be sent and summed in bfloat16 or wider, within the bound.
A program may use at most 192 MiB of HBM per device.

v0:
```python
import jax
import jax.numpy as jnp
from jax import lax
from jax.sharding import PartitionSpec as P


def from_behind(value, axis, by):
    length = lax.axis_size(axis)
    return lax.ppermute(value, axis, [(i, (i + by) % length) for i in range(length)])


def slot_tables(route_ids, node_count, capacity):
    token_count, route_count = route_ids.shape
    entries = token_count * route_count
    flat_ids = route_ids.reshape(entries)
    onehot = (flat_ids[:, None] == jnp.arange(node_count, dtype=jnp.int32)[None, :]).astype(
        jnp.int32
    )
    rank_in = jnp.cumsum(onehot, axis=0) - 1
    slot_of = jnp.sum(rank_in * onehot, axis=1)
    slot_table = jnp.full((capacity, node_count), entries, jnp.int32)
    slot_table = slot_table.at[slot_of, flat_ids].set(
        jnp.arange(entries, dtype=jnp.int32), mode="drop"
    )
    return (slot_of, flat_ids, slot_table)


def body(layer_input, out_grad, routes, gates, gate_weight, up_weight, down_weight):
    node_count = lax.axis_size("node")
    local_count = lax.axis_size("local")
    token_count = layer_input.shape[1]
    quarter = layer_input.shape[2]
    route_count = routes.shape[2]
    capacity = min(2 * token_count * route_count // node_count, 3 * token_count // 4)
    entries = token_count * route_count
    slot_of, flat_ids, slot_table = slot_tables(routes[0], node_count, capacity)
    live_slots = slot_table < entries
    entry_idx = jnp.minimum(slot_table, entries - 1)
    token_idx = entry_idx // route_count
    live_scale = live_slots.astype(jnp.bfloat16)
    send_input = layer_input[0][token_idx] * live_scale[:, :, None]
    send_grads = out_grad[0][token_idx] * live_scale[:, :, None]
    send_gates = gates[0].reshape(entries)[entry_idx] * live_scale
    wide_shape = (capacity, node_count, local_count, quarter)
    wide_input = jnp.broadcast_to(send_input[:, :, None, :], wide_shape).reshape(
        capacity, node_count * local_count, quarter
    )
    wide_grads = jnp.broadcast_to(send_grads[:, :, None, :], wide_shape).reshape(
        capacity, node_count * local_count, quarter
    )
    wide_gates = jnp.broadcast_to(
        send_gates[:, :, None], (capacity, node_count, local_count)
    ).reshape(capacity, node_count * local_count)
    got_input, got_grads, got_gates = (
        lax.all_to_all(wide_input, ("node", "local"), split_axis=1, concat_axis=1, tiled=True),
        lax.all_to_all(wide_grads, ("node", "local"), split_axis=1, concat_axis=1, tiled=True),
        lax.all_to_all(wide_gates, ("node", "local"), split_axis=1, concat_axis=1, tiled=True),
    )
    rows_input = got_input.reshape(capacity, node_count, local_count * quarter)
    rows_grads = got_grads.reshape(capacity, node_count, local_count * quarter)
    own_column = (jnp.arange(local_count, dtype=jnp.int32) == lax.axis_index("local")).astype(
        jnp.float32
    )
    row_gate = jnp.sum(
        got_gates.reshape(capacity, node_count, local_count).astype(jnp.float32) * own_column,
        axis=2,
    )
    row_total = capacity * node_count
    flat_input = rows_input.reshape(row_total, -1)
    flat_grads = rows_grads.reshape(row_total, -1)
    gate_column = row_gate.reshape(row_total, 1)
    w_gate = gate_weight[0, 0]
    w_up = up_weight[0, 0]
    w_down = down_weight[0, 0]
    pre_gate = jnp.dot(flat_input, w_gate, preferred_element_type=jnp.float32)
    pre_up = jnp.dot(flat_input, w_up, preferred_element_type=jnp.float32)
    hidden_raw = jnp.dot(flat_grads, w_down.T, preferred_element_type=jnp.float32)
    sigmoid_gate = jax.nn.sigmoid(pre_gate)
    swish_gate = pre_gate * sigmoid_gate
    activation = swish_gate * pre_up
    gate_part = jnp.sum(activation * hidden_raw, axis=1)
    gated_act = (gate_column * activation).astype(jnp.bfloat16)
    scaled = gate_column * hidden_raw
    grad_gate = (scaled * pre_up * sigmoid_gate * (1.0 + pre_gate * (1.0 - sigmoid_gate))).astype(
        jnp.bfloat16
    )
    grad_up = (scaled * swish_gate).astype(jnp.bfloat16)
    unit_terms = jnp.dot(grad_gate, w_gate.T, preferred_element_type=jnp.float32)
    unit_terms = unit_terms + jnp.dot(grad_up, w_up.T, preferred_element_type=jnp.float32)
    unit_terms = unit_terms.reshape(capacity, node_count, -1)
    gate_spread = jnp.broadcast_to(
        gate_part.reshape(capacity, node_count, 1), (capacity, node_count, local_count)
    )
    back_rows = unit_terms.astype(jnp.bfloat16).reshape(capacity, node_count * local_count, quarter)
    back_gate = gate_spread.astype(jnp.bfloat16).reshape(capacity, node_count * local_count)
    got_rows, got_gate = (
        lax.all_to_all(back_rows, ("node", "local"), split_axis=1, concat_axis=1, tiled=True),
        lax.all_to_all(back_gate, ("node", "local"), split_axis=1, concat_axis=1, tiled=True),
    )
    route_rows = jnp.sum(
        got_rows.reshape(capacity, node_count, local_count, quarter), axis=2, dtype=jnp.float32
    )
    route_rows = lax.optimization_barrier(route_rows.astype(jnp.bfloat16))
    route_gate = jnp.sum(
        got_gate.reshape(capacity, node_count, local_count), axis=2, dtype=jnp.float32
    )
    route_gate = lax.optimization_barrier(route_gate.astype(jnp.bfloat16))
    flat_rows = route_rows.reshape(capacity * node_count, quarter)
    position = jnp.minimum(slot_of * node_count + flat_ids, capacity * node_count - 1)
    per_entry = flat_rows[position].reshape(token_count, route_count, quarter)
    input_grad = jnp.sum(per_entry, axis=1, dtype=jnp.float32).astype(jnp.bfloat16)
    gate_grad = (
        route_gate.reshape(capacity * node_count)[position]
        .astype(jnp.float32)
        .reshape(1, token_count, route_count)
    )
    passed = from_behind(input_grad[None], "section", -1)
    gate_wgrad = jnp.dot(flat_input.T, grad_gate, preferred_element_type=jnp.float32).astype(
        jnp.bfloat16
    )
    up_wgrad = jnp.dot(flat_input.T, grad_up, preferred_element_type=jnp.float32).astype(
        jnp.bfloat16
    )
    down_wgrad = jnp.dot(gated_act.T, flat_grads, preferred_element_type=jnp.float32).astype(
        jnp.bfloat16
    )
    return (passed, gate_grad, gate_wgrad[None, None], up_wgrad[None, None], down_wgrad[None, None])


def solution(mesh):
    return jax.shard_map(
        body,
        mesh=mesh,
        in_specs=(
            P("section", "node", "local"),
            P("section", "node", "local"),
            P("section", "node", None),
            P("section", "node", None),
            P("section", "node", None, "local"),
            P("section", "node", None, "local"),
            P("section", "node", "local", None),
        ),
        out_specs=(
            P("section", "node", "local"),
            P("section", "node", None),
            P("section", "node", None, "local"),
            P("section", "node", None, "local"),
            P("section", "node", "local", None),
        ),
        check_vma=False,
    )
```

profile of v0, /device:TPU:0, one launch (start us, length us, event | category | flops | bytes accessed | tf_op | source)
XLA Modules:
  0.0 224.3 jit_solution(12168901015622430712)
XLA Ops:
  0.6 0.7 iota_compare_fusion
  1.4 0.6 reduce-window.6
  2.0 0.2 slice_reduce_fusion
  2.3 0.2 reduce-window.9
  2.5 0.7 fusion.17
  3.2 0.7 compare_select_fusion
  3.9 7.8 %scatter_fusion = s32[120,2]{0,1:T(2,128)S(1)} fusion(s32[120,2]{0,1:T(2,128)S(1)} %broadcast.116, s32[160]{0:T(256)S(1)} %bitcast.68, s32[160]{0:T(256)S(1)} %iota.13), kind=kCustom, calls=%fused_computation.5 | custom fusion | bytes 3200 | tf_op jit(solution)/shard_map/scatter | solution.py:22
  11.8 0.1 copy.44
  11.9 0.1 reshape.176
  12.0 0.7 reduce.3
  12.7 1.9 gather_fusion
  14.6 0.2 reshape.175
  14.8 0.1 copy.45
  14.9 0.6 copy.46
  15.5 5.2 %all-to-all-start = ((bf16[120,8,1]{0,2,1:T(2,128)(2,1)}), bf16[120,8,1]{0,2,1:T(2,128)(2,1)S(1)}, u32[]{:S(2)}, u32[]{:S(2)}) async-start(bf16[120,8,1]{0,2,1:T(2,128)(2,1)} %copy.46), calls=%async_computation | async-start | bytes 8192 | tf_op jit(solution)/shard_map/all_to_all | solution.py:57
  20.7 1.3 gather_fusion.1
  22.0 0.3 reshape.183
  22.3 1.3 gather_fusion.2
  23.6 1.2 reshape.191
  24.9 0.1 copy.49
  25.0 2.7 %broadcast_multiply_fusion.1 = (bf16[120,2,1792]{2,1,0:T(2,128)(2,1)S(1)}, bf16[120,2,1792]{2,1,0:T(2,128)(2,1)S(1)}) fusion(bf16[120,2,1792]{2,1,0:T(2,128)(2,1)S(1)} %reshape.183, bf16[120,2]{1,0:T(8,128)(2,1)S(1)} %copy.49, bf16[120,2,1792]{2,1,0:T(2,128)(2,1)} %reshape.191), kind=kLoop, calls=%fused_computation.25 | loop fusion | flops 860160 | bytes 3441120 | tf_op jit(solution)/shard_map/mul | solution.py:42
  27.7 0.1 copy.52
  27.8 2.0 broadcast_in_dim.19
  29.8 4.5 %all-to-all-start.2 = ((bf16[120,8,1792]{2,0,1:T(8,128)(2,1)}), bf16[120,8,1792]{2,0,1:T(8,128)(2,1)}, u32[]{:S(2)}, u32[]{:S(2)}) async-start(bf16[120,8,1792]{2,0,1:T(8,128)(2,1)} %bitcast.67), calls=%async_computation.2 | async-start | bytes 6881280 | tf_op jit(solution)/shard_map/all_to_all | solution.py:55
  34.3 0.1 copy.50
  34.4 41.0 %all-to-all-done.2 = bf16[120,8,1792]{2,0,1:T(8,128)(2,1)} async-done(((bf16[120,8,1792]{2,0,1:T(8,128)(2,1)}), bf16[120,8,1792]{2,0,1:T(8,128)(2,1)}, u32[]{:S(2)}, u32[]{:S(2)}) %all-to-all-start.2) | async-done | bytes 3440672 | tf_op jit(solution)/shard_map/all_to_all | solution.py:55
  75.3 2.0 broadcast_in_dim.18
  77.3 4.7 %all-to-all-start.1 = ((bf16[120,8,1792]{2,0,1:T(8,128)(2,1)}), bf16[120,8,1792]{2,0,1:T(8,128)(2,1)}, u32[]{:S(2)}, u32[]{:S(2)}) async-start(bf16[120,8,1792]{2,0,1:T(8,128)(2,1)} %bitcast.66), calls=%async_computation.1 | async-start | bytes 6881280 | tf_op jit(solution)/shard_map/all_to_all | solution.py:56
  82.0 0.1 fusion.16
  82.1 0.1 copy.48
  82.2 0.1 mul.93
  82.4 4.4 %copy.53 = bf16[120,8,1792]{2,1,0:T(8,128)(2,1)} copy(bf16[120,8,1792]{2,0,1:T(8,128)(2,1)} %all-to-all-done.2) | data formatting | bytes 6881280 | tf_op jit(solution)/shard_map/all_to_all | solution.py:55
  86.7 6.3 %reshape_reshape.7 = bf16[240,7168]{1,0:T(8,128)(2,1)} reshape(bf16[120,8,1792]{2,1,0:T(8,128)(2,1)} %copy.53) | data formatting | bytes 6881280 | tf_op jit(solution)/shard_map/reshape;reshape | solution.py:69
  93.0 4.3 %fusion.6 = f32[240,256]{1,0:T(8,128)S(1)} fusion(bf16[240,7168]{1,0:T(8,128)(2,1)} %reshape_reshape.7, bf16[1,1,7168,256]{3,2,1,0:T(8,128)(2,1)} %param.11), kind=kOutput, calls=%fused_computation.16 | convolution fusion | flops 880803840 | bytes 7356416 | tf_op jit(solution)/shard_map/dot_general | solution.py:75
  97.3 0.9 copy-done.6
  98.2 1.0 fusion.9
  99.2 23.7 %all-to-all-done.1 = bf16[120,8,1792]{2,0,1:T(8,128)(2,1)} async-done(((bf16[120,8,1792]{2,0,1:T(8,128)(2,1)}), bf16[120,8,1792]{2,0,1:T(8,128)(2,1)}, u32[]{:S(2)}, u32[]{:S(2)}) %all-to-all-start.1) | async-done | bytes 3440672 | tf_op jit(solution)/shard_map/all_to_all | solution.py:56
  122.9 4.4 %copy.51 = bf16[120,8,1792]{2,1,0:T(8,128)(2,1)} copy(bf16[120,8,1792]{2,0,1:T(8,128)(2,1)} %all-to-all-done.1) | data formatting | bytes 6881280 | tf_op jit(solution)/shard_map/all_to_all | solution.py:56
  127.2 6.3 %reshape_reshape.6 = bf16[240,7168]{1,0:T(8,128)(2,1)} reshape(bf16[120,8,1792]{2,1,0:T(8,128)(2,1)} %copy.51) | data formatting | bytes 6881280 | tf_op jit(solution)/shard_map/reshape;reshape | solution.py:70
  133.5 4.5 %multiply_reduce_fusion = (bf16[240]{0:T(256)(128)(2,1)S(1)}, bf16[240,256]{1,0:T(8,128)(2,1)S(1)}, bf16[240,256]{1,0:T(8,128)(2,1)S(1)}) fusion(f32[240,256]{1,0:T(8,128)S(1)} %fusion.9, f32[240,256]{1,0:T(8,128)S(1)} %fusion.6, f32[240]{0:T(256)S(1)} %mul.93, bf16[240,7168]{1,0:T(8,128)(2,1)} %reshape_reshape.6, bf16[1,1,256,7168]{3,2,1,0:T(8,128)(2,1)} %param.13), kind=kOutput, calls=%fused_computation.27 | convolution fusion | flops 881848064 | bytes 7849376 | tf_op jit(solution)/shard_map/dot_general | solution.py:77
  138.0 1.2 fusion.4
  139.2 0.9 copy-done.7
  140.1 3.0 %fusion = bf16[240,7168]{1,0:T(8,128)(2,1)} fusion(f32[240,7168]{1,0:T(8,128)S(1)} %fusion.4, bf16[240,256]{1,0:T(8,128)(2,1)S(1)} %get-tuple-element.7, bf16[1,1,7168,256]{3,2,1,0:T(8,128)(2,1)S(1)} %copy-done.7), kind=kOutput, calls=%fused_computation.10 | convolution fusion | flops 884244480 | bytes 14114816 | tf_op jit(solution)/shard_map/dot_general | solution.py:89
  143.1 6.3 %convert_element_type.84 = bf16[120,8,1792]{2,1,0:T(8,128)(2,1)} reshape(bf16[240,7168]{1,0:T(8,128)(2,1)} %fusion) | data formatting | bytes 6881280 | tf_op jit(solution)/shard_map/convert_element_type | solution.py:94
  149.4 4.4 %copy.54 = bf16[120,8,1792]{2,0,1:T(8,128)(2,1)} copy(bf16[120,8,1792]{2,1,0:T(8,128)(2,1)} %convert_element_type.84) | data formatting | bytes 6881280 | tf_op jit(solution)/shard_map/convert_element_type | solution.py:94
  153.7 4.5 %all-to-all-start.3 = ((bf16[120,8,1792]{2,0,1:T(8,128)(2,1)}), bf16[120,8,1792]{2,0,1:T(8,128)(2,1)}, u32[]{:S(2)}, u32[]{:S(2)}) async-start(bf16[120,8,1792]{2,0,1:T(8,128)(2,1)} %copy.54), calls=%async_computation.3 | async-start | bytes 6881280 | tf_op jit(solution)/shard_map/all_to_all | solution.py:97
  158.2 0.2 convert_element_type.86
  158.5 0.6 copy.57
  159.1 5.0 %fusion.1 = bf16[1,1,7168,256]{3,2,1,0:T(8,128)(2,1)} fusion(bf16[240,7168]{1,0:T(8,128)(2,1)} %reshape_reshape.7, bf16[240,256]{1,0:T(8,128)(2,1)S(1)} %get-tuple-element.6), kind=kOutput, calls=%fused_computation.11 | convolution fusion | flops 882638848 | bytes 7233536 | tf_op jit(solution)/shard_map/dot_general | solution.py:118
  164.1 35.2 %all-to-all-done.3 = bf16[120,8,1792]{2,0,1:T(8,128)(2,1)} async-done(((bf16[120,8,1792]{2,0,1:T(8,128)(2,1)}), bf16[120,8,1792]{2,0,1:T(8,128)(2,1)}, u32[]{:S(2)}, u32[]{:S(2)}) %all-to-all-start.3) | async-done | bytes 3440672 | tf_op jit(solution)/shard_map/all_to_all | solution.py:97
  199.3 3.5 %all-to-all-start.4 = ((bf16[120,8,1]{0,2,1:T(2,128)(2,1)}), bf16[120,8,1]{0,2,1:T(2,128)(2,1)S(1)}, u32[]{:S(2)}, u32[]{:S(2)}) async-start(bf16[120,8,1]{0,2,1:T(2,128)(2,1)} %copy.57), calls=%async_computation.4 | async-start | bytes 8192 | tf_op jit(solution)/shard_map/all_to_all | solution.py:98
  202.8 2.4 %bitcast_reduce_fusion = bf16[120,2,1792]{2,0,1:T(8,128)(2,1)S(1)} fusion(bf16[120,8,1792]{2,0,1:T(8,128)(2,1)} %all-to-all-done.3), kind=kLoop, calls=%fused_computation.23 | loop fusion | flops 1290240 | bytes 4300800 | tf_op jit(solution)/shard_map/reduce_sum | solution.py:100
  205.2 0.7 copy.55
  205.9 0.3 reshape.168
  206.2 1.0 gather_fusion.3
  207.3 3.7 %collective-permute-start = (bf16[1,160,1792]{2,1,0:T(8,128)(2,1)S(1)}, bf16[1,160,1792]{2,1,0:T(8,128)(2,1)S(1)}, u32[]{:S(2)}, u32[]{:S(2)}) collective-permute-start(bf16[1,160,1792]{2,1,0:T(8,128)(2,1)S(1)} %bitcast.69), channel_id=1, source_target_pairs={{0,24},{8,0},{16,8},{24,16},{1,25},{9,1},{17,9},{25,17},{2,26},{10... | collective-permute-start | bytes 1720328 | tf_op jit(solution)/shard_map/ppermute | solution.py:9
  211.0 5.1 %fusion.2 = bf16[1,1,7168,256]{3,2,1,0:T(8,128)(2,1)} fusion(bf16[240,7168]{1,0:T(8,128)(2,1)} %reshape_reshape.7, bf16[240,256]{1,0:T(8,128)(2,1)S(1)} %get-tuple-element.7), kind=kOutput, calls=%fused_computation.12 | convolution fusion | flops 882638848 | bytes 7233536 | tf_op jit(solution)/shard_map/dot_general | solution.py:121
  216.0 3.1 %fusion.3 = bf16[1,1,256,7168]{3,2,1,0:T(8,128)(2,1)} fusion(bf16[240,7168]{1,0:T(8,128)(2,1)S(1)} %copy-done.4, f32[240]{0:T(256)S(1)} %mul.93, f32[240,256]{1,0:T(8,128)S(1)} %fusion.9, f32[240,256]{1,0:T(8,128)S(1)} %fusion.6), kind=kOutput, calls=%fused_computation.13 | convolution fusion | flops 883068928 | bytes 7603136 | tf_op jit(solution)/shard_map/dot_general | solution.py:124
  219.1 0.1 copy.58
  219.3 0.1 reshape.170
  219.4 1.6 gather_fusion.4
  221.0 0.6 convert_element_type.94
  221.5 2.0 collective-permute-done
  223.5 0.8 copy.65
  (34 shorter events, 0.3 us)
Async XLA Ops:
  0.6 20.0 %copy-start = (bf16[1,160,1792]{2,1,0:T(8,128)(2,1)S(1)}, bf16[1,160,1792]{2,1,0:T(8,128)(2,1)}, u32[]{:S(2)}) copy-start(bf16[1,160,1792]{2,1,0:T(8,128)(2,1)} %param.8) | copy-start | bytes 1720324
  15.5 12.3 %all-to-all-start = ((bf16[120,8,1]{0,2,1:T(2,128)(2,1)}), bf16[120,8,1]{0,2,1:T(2,128)(2,1)S(1)}, u32[]{:S(2)}, u32[]{:S(2)}) async-start(bf16[120,8,1]{0,2,1:T(2,128)(2,1)} %copy.46), calls=%async_computation | async-start | bytes 8192 | tf_op jit(solution)/shard_map/all_to_all | solution.py:57
  20.7 1.6 copy-start.2
  29.8 45.5 %all-to-all-start.2 = ((bf16[120,8,1792]{2,0,1:T(8,128)(2,1)}), bf16[120,8,1792]{2,0,1:T(8,128)(2,1)}, u32[]{:S(2)}, u32[]{:S(2)}) async-start(bf16[120,8,1792]{2,0,1:T(8,128)(2,1)} %bitcast.67), calls=%async_computation.2 | async-start | bytes 6881280 | tf_op jit(solution)/shard_map/all_to_all | solution.py:55
  77.3 45.6 %all-to-all-start.1 = ((bf16[120,8,1792]{2,0,1:T(8,128)(2,1)}), bf16[120,8,1792]{2,0,1:T(8,128)(2,1)}, u32[]{:S(2)}, u32[]{:S(2)}) async-start(bf16[120,8,1792]{2,0,1:T(8,128)(2,1)} %bitcast.66), calls=%async_computation.1 | async-start | bytes 6881280 | tf_op jit(solution)/shard_map/all_to_all | solution.py:56
  93.0 4.3 %copy-start.3 = (bf16[240,7168]{1,0:T(8,128)(2,1)S(1)}, bf16[240,7168]{1,0:T(8,128)(2,1)}, u32[]{:S(2)}) copy-start(bf16[240,7168]{1,0:T(8,128)(2,1)} %reshape_reshape.7) | copy-start | bytes 10321924
  93.0 5.2 %copy-start.6 = (bf16[1,1,7168,256]{3,2,1,0:T(8,128)(2,1)S(1)}, bf16[1,1,7168,256]{3,2,1,0:T(8,128)(2,1)}, u32[]{:S(2)}) copy-start(bf16[1,1,7168,256]{3,2,1,0:T(8,128)(2,1)} %param.12) | copy-start | bytes 11010052
  133.5 4.5 %copy-start.5 = (bf16[1,1,7168,256]{3,2,1,0:T(8,128)(2,1)S(1)}, bf16[1,1,7168,256]{3,2,1,0:T(8,128)(2,1)}, u32[]{:S(2)}) copy-start(bf16[1,1,7168,256]{3,2,1,0:T(8,128)(2,1)} %param.11) | copy-start | bytes 11010052
  138.0 2.0 copy-start.7
  153.7 45.5 %all-to-all-start.3 = ((bf16[120,8,1792]{2,0,1:T(8,128)(2,1)}), bf16[120,8,1792]{2,0,1:T(8,128)(2,1)}, u32[]{:S(2)}, u32[]{:S(2)}) async-start(bf16[120,8,1792]{2,0,1:T(8,128)(2,1)} %copy.54), calls=%async_computation.3 | async-start | bytes 6881280 | tf_op jit(solution)/shard_map/all_to_all | solution.py:97
  199.3 19.8 %all-to-all-start.4 = ((bf16[120,8,1]{0,2,1:T(2,128)(2,1)}), bf16[120,8,1]{0,2,1:T(2,128)(2,1)S(1)}, u32[]{:S(2)}, u32[]{:S(2)}) async-start(bf16[120,8,1]{0,2,1:T(2,128)(2,1)} %copy.57), calls=%async_computation.4 | async-start | bytes 8192 | tf_op jit(solution)/shard_map/all_to_all | solution.py:98
  207.3 8.7 %copy-start.4 = (bf16[240,7168]{1,0:T(8,128)(2,1)S(1)}, bf16[240,7168]{1,0:T(8,128)(2,1)}, u32[]{:S(2)}) copy-start(bf16[240,7168]{1,0:T(8,128)(2,1)} %reshape_reshape.6) | copy-start | bytes 10321924
  207.3 16.2 %collective-permute-start = (bf16[1,160,1792]{2,1,0:T(8,128)(2,1)S(1)}, bf16[1,160,1792]{2,1,0:T(8,128)(2,1)S(1)}, u32[]{:S(2)}, u32[]{:S(2)}) collective-permute-start(bf16[1,160,1792]{2,1,0:T(8,128)(2,1)S(1)} %bitcast.69), channel_id=1, source_target_pairs={{0,24},{8,0},{16,8},{24,16},{1,25},{9,1},{17,9},{25,17},{2,26},{10... | collective-permute-start | bytes 1720328 | tf_op jit(solution)/shard_map/ppermute | solution.py:9
  210.9 13.4 %copy-start.1 = (bf16[1,160,1792]{2,1,0:T(8,128)(2,1)S(1)}, bf16[1,160,1792]{2,1,0:T(8,128)(2,1)}, u32[]{:S(2)}) copy-start(bf16[1,160,1792]{2,1,0:T(8,128)(2,1)} %param.8) | copy-start | bytes 1720324
where the time goes:
time: 225 us; the launch traced here: 224 us
  waiting for transfers between devices  102 us (45%)
  local copies, waits for them, and re-layouts  58.9 us (26%)
  matrix products  27.2 us (12%)
  starting transfers between devices  26 us (12%)
  other arithmetic  9.58 us (4%)
    all_to_all x1, waiting for transfers between devices, body(): lax.all_to_all(wide_input, ('node', 'local'), split_axis=1, concat_axis=1...  41 us
    all_to_all x1, waiting for transfers between devices, body(): lax.all_to_all(back_rows, ('node', 'local'), split_axis=1, concat_axis=1,...  35.2 us
    all_to_all x1, waiting for transfers between devices, body(): lax.all_to_all(wide_grads, ('node', 'local'), split_axis=1, concat_axis=1...  23.7 us
    convert_element_type x2, local copies, waits for them, and re-layouts, body(): unit_terms.astype(jnp.bfloat16)  10.6 us
    scatter x1, local copies, waits for them, and re-layouts, slot_tables(): slot_table.at[slot_of, flat_ids]  7.82 us
    another operation x1, local copies, waits for them, and re-layouts, body(): flat_input = rows_input.reshape(row_total, -1)  6.27 us
    another operation x1, local copies, waits for them, and re-layouts, body(): flat_grads = rows_grads.reshape(row_total, -1)  6.26 us
    all_to_all x1, starting transfers between devices, body(): lax.all_to_all(wide_gates, ('node', 'local'), split_axis=1, concat_axis=1...  5.17 us
  transfers between devices with their start and end apart: 6, of which 4 were waited for; matrix products, arithmetic and copies ran while one was open for 20% of the time, Pallas kernels for 0%

commit v1 on v0

v1 whole, which is shorter than its diff:
```python
import functools

import jax
import jax.numpy as jnp
from jax import lax
from jax.experimental import pallas as pl
from jax.experimental.pallas import tpu as pltpu
from jax.sharding import PartitionSpec as P

F32 = jnp.float32
BF16 = jnp.bfloat16
MESH = pl.DeviceIdType.MESH
NT = (((1,), (1,)), ((), ()))
TN = (((0,), (0,)), ((), ()))


def from_behind(value, axis, by):
    length = lax.axis_size(axis)
    return lax.ppermute(value, axis, [(i, (i + by) % length) for i in range(length)])


def slot_tables(route_ids, node_count, capacity):
    token_count, route_count = route_ids.shape
    entries = token_count * route_count
    flat_ids = route_ids.reshape(entries)
    order = jnp.arange(entries, dtype=jnp.int32)
    earlier = (order[None, :] < order[:, None]) & (flat_ids[None, :] == flat_ids[:, None])
    slot_of = jnp.sum(earlier.astype(jnp.int32), axis=1)
    slot_table = jnp.full((capacity, node_count), entries, jnp.int32)
    slot_table = slot_table.at[slot_of, flat_ids].set(order, mode="drop")
    return (slot_of, flat_ids, slot_table)


def general_body(layer_input, out_grad, routes, gates, gate_weight, up_weight, down_weight):
    node_count = lax.axis_size("node")
    local_count = lax.axis_size("local")
    token_count = layer_input.shape[1]
    quarter = layer_input.shape[2]
    route_count = routes.shape[2]
    capacity = min(2 * token_count * route_count // node_count, 3 * token_count // 4)
    entries = token_count * route_count
    slot_of, flat_ids, slot_table = slot_tables(routes[0], node_count, capacity)
    live_slots = slot_table < entries
    entry_idx = jnp.minimum(slot_table, entries - 1)
    token_idx = entry_idx // route_count
    live_scale = live_slots.astype(BF16)
    send_input = layer_input[0][token_idx] * live_scale[:, :, None]
    send_grads = out_grad[0][token_idx] * live_scale[:, :, None]
    send_gates = gates[0].reshape(entries)[entry_idx] * live_scale
    wide_shape = (capacity, node_count, local_count, quarter)

    def exchange(value):
        return lax.all_to_all(value, ("node", "local"), split_axis=1, concat_axis=1, tiled=True)

    def widen(value):
        wide = jnp.broadcast_to(value[:, :, None, :], wide_shape)
        return wide.reshape(capacity, node_count * local_count, quarter)

    wide_gates = jnp.broadcast_to(send_gates[:, :, None], wide_shape[:3])
    got_input = exchange(widen(send_input))
    got_grads = exchange(widen(send_grads))
    got_gates = exchange(wide_gates.reshape(capacity, node_count * local_count))
    row_total = capacity * node_count
    flat_input = got_input.reshape(row_total, -1)
    flat_grads = got_grads.reshape(row_total, -1)
    own_column = (jnp.arange(local_count, dtype=jnp.int32) == lax.axis_index("local")).astype(F32)
    gate_column = jnp.sum(
        got_gates.reshape(capacity, node_count, local_count).astype(F32) * own_column, axis=2
    ).reshape(row_total, 1)
    w_gate = gate_weight[0, 0]
    w_up = up_weight[0, 0]
    w_down = down_weight[0, 0]
    pre_gate = jnp.dot(flat_input, w_gate, preferred_element_type=F32)
    pre_up = jnp.dot(flat_input, w_up, preferred_element_type=F32)
    hidden_raw = jnp.dot(flat_grads, w_down.T, preferred_element_type=F32)
    gate_part, gated_act, grad_gate, grad_up = unit_math(pre_gate, pre_up, hidden_raw, gate_column)
    unit_terms = jnp.dot(grad_gate, w_gate.T, preferred_element_type=F32)
    unit_terms = unit_terms + jnp.dot(grad_up, w_up.T, preferred_element_type=F32)
    gate_spread = jnp.broadcast_to(gate_part.reshape(capacity, node_count, 1), wide_shape[:3])
    got_rows = exchange(unit_terms.astype(BF16).reshape(capacity, node_count * local_count, quarter))
    got_gate = exchange(gate_spread.astype(BF16).reshape(capacity, node_count * local_count))
    route_rows = jnp.sum(got_rows.reshape(wide_shape), axis=2, dtype=F32)
    route_rows = lax.optimization_barrier(route_rows.astype(BF16))
    route_gate = jnp.sum(got_gate.reshape(wide_shape[:3]), axis=2, dtype=F32)
    route_gate = lax.optimization_barrier(route_gate.astype(BF16))
    flat_rows = route_rows.reshape(row_total, quarter)
    position = jnp.minimum(slot_of * node_count + flat_ids, row_total - 1)
    per_entry = flat_rows[position].reshape(token_count, route_count, quarter)
    input_grad = jnp.sum(per_entry, axis=1, dtype=F32).astype(BF16)
    gate_grad = (
        route_gate.reshape(row_total)[position].astype(F32).reshape(1, token_count, route_count)
    )
    passed = from_behind(input_grad[None], "section", -1)
    gate_wgrad = jnp.dot(flat_input.T, grad_gate, preferred_element_type=F32).astype(BF16)
    up_wgrad = jnp.dot(flat_input.T, grad_up, preferred_element_type=F32).astype(BF16)
    down_wgrad = jnp.dot(gated_act.T, flat_grads, preferred_element_type=F32).astype(BF16)
    return (passed, gate_grad, gate_wgrad[None, None], up_wgrad[None, None], down_wgrad[None, None])


def unit_math(pre_gate, pre_up, hidden_raw, gate_column):
    sigmoid_gate = jax.nn.sigmoid(pre_gate)
    swish_gate = pre_gate * sigmoid_gate
    activation = swish_gate * pre_up
    gate_part = jnp.sum(activation * hidden_raw, axis=1, keepdims=True)
    gated_act = (gate_column * activation).astype(BF16)
    scaled = gate_column * hidden_raw
    grad_gate = (scaled * pre_up * sigmoid_gate * (1.0 + pre_gate * (1.0 - sigmoid_gate))).astype(
        BF16
    )
    grad_up = (scaled * swish_gate).astype(BF16)
    return gate_part, gated_act, grad_gate, grad_up


def layer_kernel(
    T, K, C, F,
    x_ref, dy_ref, routes_ref, gates_ref, wg_hbm, wu_hbm, wd_hbm,
    ig_ref, gate_out_ref, gg_ref, gu_ref, ga_ref, rx_hbm, rd_hbm,
    wg, wu, wd, pick, xf, rx, rd, xs, dys, gsend, grecv, pg, pu, hr,
    sa, ra, sb, rb, own, sc, rc, gts, gtr,
    send_sem, recv_sem, load_sem, out_sem,
):
    n = lax.axis_index("node")
    l = lax.axis_index("local")
    xi = l // 2
    ci = l % 2
    q_me = l
    q_xm = 2 * (1 - xi) + ci
    q_cm = 2 * xi + 1 - ci
    q_cx = 2 * (1 - xi) + 1 - ci
    x_mate = {"local": q_xm}
    c_mate = {"local": q_cm}
    y_mate = {"node": 1 - n}

    loads = [
        pltpu.make_async_copy(wg_hbm, wg, load_sem.at[0]),
        pltpu.make_async_copy(wu_hbm, wu, load_sem.at[1]),
    ]
    for q in range(4):
        loads.append(
            pltpu.make_async_copy(wd_hbm.at[:, pl.ds(q * C, C)], wd.at[q], load_sem.at[2 + q])
        )

    barrier = pltpu.get_barrier_semaphore()
    for dn in range(2):
        for dl in range(4):
            if dn or dl:
                pl.semaphore_signal(
                    barrier, inc=1, device_id_type=MESH,
                    device_id={"node": lax.rem(n + dn, 2), "local": lax.rem(l + dl, 4)},
                )
    pl.semaphore_wait(barrier, 7)

    sent = []

    def send(i, src, dst, dev):
        d = pltpu.make_async_remote_copy(
            src_ref=src, dst_ref=dst, send_sem=send_sem.at[i], recv_sem=recv_sem.at[i],
            device_id=dev, device_id_type=MESH,
        )
        d.start()
        sent.append(d)
        return d

    m0 = send(0, x_ref, xf.at[q_me], x_mate)

    ids = routes_ref[...]
    before = lax.broadcasted_iota(jnp.int32, (T, T), 0) < lax.broadcasted_iota(jnp.int32, (T, T), 1)
    before = jnp.where(before, 1.0, 0.0).astype(BF16)
    slot = lax.broadcasted_iota(jnp.int32, (K, T), 0).astype(F32)
    gate_row = gates_ref[...].astype(F32)
    columns = []
    for g in range(2):
        named = jnp.where(ids == (n if g == 0 else 1 - n), 1.0, 0.0)
        rank = jnp.dot(
            jnp.broadcast_to(named, (16, T)).astype(BF16), before, preferred_element_type=F32
        )[0:1]
        hit = jnp.where(rank == slot, jnp.broadcast_to(named, (K, T)), 0.0)
        pick[g] = hit.astype(BF16)
        columns.append(jnp.sum(hit * gate_row, axis=1, keepdims=True))

    def select(g, rows):
        return jnp.dot(pick[g], rows, preferred_element_type=F32).astype(BF16)

    dys[...] = select(1, dy_ref[...])
    m3 = send(3, dys, rd.at[q_me, 1], y_mate)
    gsend[...] = jnp.broadcast_to(columns[1], (K, 128)).astype(BF16)
    m14 = send(14, gsend, grecv, y_mate)
    rd[q_me, 0] = select(0, dy_ref[...])
    m4 = send(4, rd.at[q_me, 0], rd.at[q_me, 0], x_mate)
    xs[0] = select(1, x_ref[...])
    m10 = send(10, xs.at[0], rx.at[q_me, 1], y_mate)
    m5 = send(5, rd.at[q_me, 0], rd.at[q_me, 0], c_mate)
    m1 = send(1, x_ref, xf.at[q_me], c_mate)
    for d in loads:
        d.start()
    rx[q_me, 0] = select(0, x_ref[...])

    m0.wait_recv()
    xs[1] = select(1, xf[q_xm])
    m11 = send(11, xs.at[1], rx.at[q_xm, 1], y_mate)
    m2 = send(2, xf.at[q_xm], xf.at[q_xm], c_mate)
    m3.wait_recv()
    m7 = send(7, rd.at[q_me, 1], rd.at[q_me, 1], x_mate)
    m8 = send(8, rd.at[q_me, 1], rd.at[q_me, 1], c_mate)
    rx[q_xm, 0] = select(0, xf[q_xm])
    m1.wait_recv()
    rx[q_cm, 0] = select(0, xf[q_cm])
    m4.wait_recv()
    m6 = send(6, rd.at[q_xm, 0], rd.at[q_xm, 0], c_mate)
    m10.wait_recv()
    m12 = send(12, rx.at[q_me, 1], rx.at[q_me, 1], c_mate)
    m2.wait_recv()
    rx[q_cx, 0] = select(0, xf[q_cx])

    for d in loads:
        d.wait()
    pg[...] = jnp.zeros_like(pg)
    pu[...] = jnp.zeros_like(pu)
    hr[...] = jnp.zeros_like(hr)

    def project(q):
        rows = rx[q].reshape(2 * K, C)
        pg[...] += jnp.dot(rows, wg[q], preferred_element_type=F32)
        pu[...] += jnp.dot(rows, wu[q], preferred_element_type=F32)

    def hidden(q):
        rows = rd[q].reshape(2 * K, C)
        hr[...] += lax.dot_general(rows, wd[q], NT, preferred_element_type=F32)

    project(q_me)
    m12.wait_recv()
    project(q_cm)
    m5.wait_recv()
    m8.wait_recv()
    m6.wait_recv()
    hidden(q_me)
    hidden(q_cm)
    m7.wait_recv()
    m9 = send(9, rd.at[q_xm, 1], rd.at[q_xm, 1], c_mate)
    m11.wait_recv()
    m13 = send(13, rx.at[q_xm, 1], rx.at[q_xm, 1], c_mate)
    hidden(q_xm)
    project(q_xm)
    m9.wait_recv()
    hidden(q_cx)
    m13.wait_recv()
    project(q_cx)
    out_copies = [
        pltpu.make_async_copy(rx, rx_hbm, out_sem.at[0]),
        pltpu.make_async_copy(rd, rd_hbm, out_sem.at[1]),
    ]
    for d in out_copies:
        d.start()
    m14.wait_recv()

    parts = []
    for g in range(2):
        rows = pl.ds(g * K, K)
        column = columns[0] if g == 0 else grecv[:, 0:1].astype(F32)
        part, act, d_gate, d_up = unit_math(pg[rows], pu[rows], hr[rows], column)
        ga_ref[rows] = act
        gg_ref[rows] = d_gate
        gu_ref[rows] = d_up
        parts.append(part)

    def terms(q, store):
        @pl.loop(0, C // 256)
        def _(j):
            at = pl.ds(pl.multiple_of(j * 256, 256), 256)
            t = lax.dot_general(gg_ref[...], wg[q, at], NT, preferred_element_type=F32)
            t += lax.dot_general(gu_ref[...], wu[q, at], NT, preferred_element_type=F32)
            t = t.astype(BF16)
            for g in range(2):
                store[g, :, at] = t[g * K : (g + 1) * K]

    terms(q_cx, sa.at[0])
    a0 = send(15, sa.at[0], ra.at[0], c_mate)
    terms(q_xm, sb)
    a0.wait_recv()
    b = [None, None]
    for g in (1, 0):
        sb[g] = (sb[g].astype(F32) + ra[0, g].astype(F32)).astype(BF16)
        b[g] = send(17 + g, sb.at[g], rb.at[g], x_mate)
    terms(q_cm, sa.at[1])
    a1 = send(16, sa.at[1], ra.at[1], c_mate)
    terms(q_me, own)

    eye = lax.broadcasted_iota(jnp.int32, (K, K), 0) == lax.broadcasted_iota(jnp.int32, (K, K), 1)
    for g in range(2):
        part = parts[g].astype(BF16).astype(F32)
        row = jnp.sum(jnp.where(eye, part, 0.0), axis=0, keepdims=True)
        gts[g] = jnp.broadcast_to(row, (16, K)).astype(BF16)
    gtr[l] = gts[0]
    gate_sent = []
    for k in range(1, 4):
        gate_sent.append(send(20 + k, gts.at[0], gtr.at[l], {"local": lax.rem(l + k, 4)}))
    for k in range(4):
        gate_sent.append(
            send(24 + k, gts.at[1], gtr.at[4 + l], {"node": 1 - n, "local": lax.rem(l + k, 4)})
        )

    a1.wait_recv()
    b[1].wait_recv()
    sc[...] = (own[1].astype(F32) + ra[1, 1].astype(F32) + rb[1].astype(F32)).astype(BF16)
    c = send(19, sc, rc, y_mate)
    for d in gate_sent:
        d.wait_recv()
    total = jnp.zeros((16, T), F32)
    for g in range(2):
        row = gtr[4 * g].astype(F32)
        for k in range(1, 4):
            row += gtr[4 * g + k].astype(F32)
        total += jnp.dot(row.astype(BF16), pick[g], preferred_element_type=F32)
    gate_out_ref[...] = total[0:1]

    b[0].wait_recv()
    own[0] = (own[0].astype(F32) + ra[1, 0].astype(F32) + rb[0].astype(F32)).astype(BF16)
    c.wait_recv()

    @pl.loop(0, C // 256)
    def _(j):
        at = pl.ds(pl.multiple_of(j * 256, 256), 256)
        t = lax.dot_general(pick[0], own[0, :, at], TN, preferred_element_type=F32)
        t += lax.dot_general(pick[1], rc[:, at], TN, preferred_element_type=F32)
        ig_ref[:, at] = t.astype(BF16)

    for d in sent:
        d.wait_send()
    for d in out_copies:
        d.wait()


def wgrad_kernel(rx_ref, rd_ref, gg_ref, gu_ref, ga_ref, gw_ref, uw_ref, dw_ref):
    rows = rx_ref[0]
    gw_ref[...] = lax.dot_general(rows, gg_ref[...], TN, preferred_element_type=F32).astype(BF16)
    uw_ref[...] = lax.dot_general(rows, gu_ref[...], TN, preferred_element_type=F32).astype(BF16)
    dw_ref[...] = lax.dot_general(
        ga_ref[...], rd_ref[0], TN, preferred_element_type=F32
    ).astype(BF16)


def fused_body(layer_input, out_grad, routes, gates, gate_weight, up_weight, down_weight):
    T, C = layer_input.shape[1:]
    D, F = gate_weight.shape[2:]
    K = -(-(3 * T // 4) // 128) * 128
    vmem = pl.BlockSpec(memory_space=pltpu.VMEM)
    hbm = pl.BlockSpec(memory_space=pl.ANY)
    shape = jax.ShapeDtypeStruct
    rows = (4, 2, K, C)
    ig, gate_grad, gg, gu, ga, rx, rd = pl.pallas_call(
        functools.partial(layer_kernel, T, K, C, F),
        out_shape=(
            shape((T, C), BF16), shape((1, T), F32),
            shape((2 * K, F), BF16), shape((2 * K, F), BF16), shape((2 * K, F), BF16),
            shape(rows, BF16), shape(rows, BF16),
        ),
        in_specs=[vmem] * 4 + [hbm] * 3,
        out_specs=(vmem,) * 5 + (hbm,) * 2,
        scratch_shapes=[
            pltpu.VMEM((4, C, F), BF16), pltpu.VMEM((4, C, F), BF16), pltpu.VMEM((4, F, C), BF16),
            pltpu.VMEM((2, K, T), BF16), pltpu.VMEM((4, T, C), BF16),
            pltpu.VMEM(rows, BF16), pltpu.VMEM(rows, BF16),
            pltpu.VMEM((2, K, C), BF16), pltpu.VMEM((K, C), BF16),
            pltpu.VMEM((K, 128), BF16), pltpu.VMEM((K, 128), BF16),
            pltpu.VMEM((2 * K, F), F32), pltpu.VMEM((2 * K, F), F32), pltpu.VMEM((2 * K, F), F32),
            pltpu.VMEM((2, 2, K, C), BF16), pltpu.VMEM((2, 2, K, C), BF16),
            pltpu.VMEM((2, K, C), BF16), pltpu.VMEM((2, K, C), BF16), pltpu.VMEM((2, K, C), BF16),
            pltpu.VMEM((K, C), BF16), pltpu.VMEM((K, C), BF16),
            pltpu.VMEM((2, 16, K), BF16), pltpu.VMEM((8, 16, K), BF16),
            pltpu.SemaphoreType.DMA((28,)), pltpu.SemaphoreType.DMA((28,)),
            pltpu.SemaphoreType.DMA((6,)), pltpu.SemaphoreType.DMA((2,)),
        ],
        compiler_params=pltpu.CompilerParams(
            collective_id=0, has_side_effects=True, vmem_limit_bytes=52 * 2**20
        ),
        name="layer",
    )(
        layer_input[0], out_grad[0], routes.reshape(1, T), gates.reshape(1, T),
        gate_weight.reshape(4, C, F), up_weight.reshape(4, C, F), down_weight.reshape(F, D),
    )
    passed = from_behind(ig[None], "section", -1)
    half = C // 2
    slab = pl.BlockSpec((1, 2 * K, half), lambda i: (i // 2, 0, i % 2))
    units = pl.BlockSpec((2 * K, F), lambda i: (0, 0))
    tall = pl.BlockSpec((half, F), lambda i: (i, 0))
    wide = pl.BlockSpec((F, half), lambda i: (0, i))
    gw, uw, dw = pl.pallas_call(
        wgrad_kernel,
        grid=(8,),
        out_shape=(shape((D, F), BF16), shape((D, F), BF16), shape((F, D), BF16)),
        in_specs=[slab, slab, units, units, units],
        out_specs=(tall, tall, wide),
        compiler_params=pltpu.CompilerParams(vmem_limit_bytes=24 * 2**20),
        cost_estimate=pl.CostEstimate(
            flops=12 * K * D * F, bytes_accessed=8 * K * D + 6 * D * F, transcendentals=0
        ),
        name="wgrad",
    )(rx.reshape(4, 2 * K, C), rd.reshape(4, 2 * K, C), gg, gu, ga)
    return (
        passed, gate_grad.reshape(1, T, 1), gw[None, None], uw[None, None], dw[None, None]
    )


def body(*args):
    routes, gate_weight = args[2], args[4]
    small = lax.axis_size("node") == 2 and lax.axis_size("local") == 4
    if small and routes.shape[2] == 1 and gate_weight.shape[1] == 1:
        return fused_body(*args)
    return general_body(*args)


def solution(mesh):
    return jax.shard_map(
        body,
        mesh=mesh,
        in_specs=(
            P("section", "node", "local"),
            P("section", "node", "local"),
            P("section", "node", None),
            P("section", "node", None),
            P("section", "node", None, "local"),
            P("section", "node", None, "local"),
            P("section", "node", "local", None),
        ),
        out_specs=(
            P("section", "node", "local"),
            P("section", "node", None),
            P("section", "node", None, "local"),
            P("section", "node", None, "local"),
            P("section", "node", "local", None),
        ),
        check_vma=False,
    )
```

time: 225 us -> 91.4 us (0.41)
  waiting for transfers between devices: 102 us -> 0.91 us
  Pallas kernels: 0 us -> 78 us
  local copies, waits for them, and re-layouts: 58.9 us -> 7.86 us
  matrix products: 27.2 us -> 0 us
  starting transfers between devices: 26 us -> 3.67 us
  other arithmetic: 9.58 us -> 0 us
    all_to_all x5 -> x0, waiting for transfers between devices: 99.8 us -> none  [the longest x1 41 us: body(): lax.all_to_all(wide_input, ('node', 'local'), split_axis=1, concat_axis=1...]
    pallas_call x0 -> x2, Pallas kernels: none -> 78 us  [the longest x1 70.9 us: fused_body(): pl.pallas_call(functools.partial(layer_kernel, T, K, C, F), out_shape=(sh...]
    dot_general x8 -> x0, matrix products: 27.2 us -> none  [the longest x1 5.07 us: body(): jnp.dot(flat_input.T, grad_up, preferred_element_type=jnp.float32)]
    all_to_all x5 -> x0, starting transfers between devices: 22.3 us -> none  [the longest x1 5.17 us: body(): lax.all_to_all(wide_gates, ('node', 'local'), split_axis=1, concat_axis=1...]
    another operation x4 -> x0, local copies, waits for them, and re-layouts: 12.6 us -> none  [the longest x1 6.27 us: body(): flat_input = rows_input.reshape(row_total, -1)]
    convert_element_type x5 -> x0, local copies, waits for them, and re-layouts: 11 us -> none  [the longest x2 10.6 us: body(): unit_terms.astype(jnp.bfloat16)]
    all_to_all x5 -> x0, local copies, waits for them, and re-layouts: 9.95 us -> none  [the longest x1 4.36 us: body(): lax.all_to_all(wide_input, ('node', 'local'), split_axis=1, concat_axis=1...]
    gather x9 -> x0, local copies, waits for them, and re-layouts: 8.85 us -> none  [the longest x2 2.52 us: body(): send_input = layer_input[0][token_idx] * live_scale[:, :, None]]
  transfers between devices with their start and end apart: 6 -> 1, of which waited for: 4 -> 1; matrix products, arithmetic and copies ran while one was open for 20% -> 0% of each run, Pallas kernels for 0% -> 8%
where the time goes in v1:
time: 91.4 us; the launch traced here: 91.1 us
  Pallas kernels  78 us (85%)
  local copies, waits for them, and re-layouts  7.86 us (9%)
  starting transfers between devices  3.67 us (4%)
    pallas_call x1, Pallas kernels, fused_body(): pl.pallas_call(functools.partial(layer_kernel, T, K, C, F), out_shape=(sh...  70.9 us
    unnamed x12, local copies, waits for them, and re-layouts  7.86 us
    pallas_call x1, Pallas kernels, fused_body(): pl.pallas_call(wgrad_kernel, grid=(8,), out_shape=(shape((D, F), BF16), s...  7.03 us
    ppermute x1, starting transfers between devices, from_behind(): lax.ppermute(value, axis, [(i, (i + by) % length) for i in range(length)])  3.67 us
  transfers between devices with their start and end apart: 1, of which 1 were waited for; matrix products, arithmetic and copies ran while one was open for 0% of the time, Pallas kernels for 8%

profile of v1, /device:TPU:0, one launch (start us, length us, event | category | flops | bytes accessed | tf_op | source)
XLA Modules:
  0.0 91.1 jit_solution(12391007116819262383)
XLA Ops:
  0.6 0.0 copy-start
  0.6 1.1 %copy-done = bf16[1,160,1792]{2,1,0:T(8,128)(2,1)S(1)} copy-done((bf16[1,160,1792]{2,1,0:T(8,128)(2,1)S(1)}, bf16[1,160,1792]{2,1,0:T(8,128)(2,1)}, u32[]{:S(2)}) %copy-start) | copy-done | bytes 573464
  1.7 0.0 copy-start.1
  1.7 0.7 copy-done.1
  2.4 0.0 copy-start.2
  2.4 0.7 copy-done.2
  3.1 70.9 %layer.1 = (bf16[160,1792]{1,0:T(8,128)(2,1)S(1)}, f32[1,160]{1,0:T(1,128)S(1)}, bf16[256,256]{1,0:T(8,128)(2,1)S(1)}, bf16[256,256]{1,0:T(8,128)(2,1)S(1)}, bf1...) custom-call(bf16[160,1792]{1,0:T(8,128)(2,1)S(1)} %bitcast.14, ...), custom_call_target="tpu_custom_call" | custom-call | tf_op jit(solution)/shard_map/layer/pallas_call | solution.py:350
  74.0 3.7 %collective-permute-start = (bf16[1,160,1792]{2,1,0:T(8,128)(2,1)S(1)}, bf16[1,160,1792]{2,1,0:T(8,128)(2,1)S(1)}, u32[]{:S(2)}, u32[]{:S(2)}) collective-permute-start(bf16[1,160,1792]{2,1,0:T(8,128)(2,1)S(1)} %bitcast.20), channel_id=1, source_target_pairs={{0,24},{8,0},{16,8},{24,16},{1,25},{9,1},{17,9},{25,17},{2,26},{10... | collective-permute-start | bytes 1720328 | tf_op jit(solution)/shard_map/ppermute | solution.py:19
  77.7 0.0 copy-start.3
  77.7 2.0 %copy-done.3 = bf16[4,2,128,1792]{3,2,1,0:T(8,128)(2,1)S(1)} copy-done((bf16[4,2,128,1792]{3,2,1,0:T(8,128)(2,1)S(1)}, bf16[4,2,128,1792]{3,2,1,0:T(8,128)(2,1)}, u32[]{:S(2)}) %copy-start.3) | copy-done | bytes 3670040
  79.7 0.0 copy-start.4
  79.7 2.0 %copy-done.4 = bf16[4,2,128,1792]{3,2,1,0:T(8,128)(2,1)S(1)} copy-done((bf16[4,2,128,1792]{3,2,1,0:T(8,128)(2,1)S(1)}, bf16[4,2,128,1792]{3,2,1,0:T(8,128)(2,1)}, u32[]{:S(2)}) %copy-start.4) | copy-done | bytes 3670040
  81.7 7.0 %wgrad.1 = (bf16[7168,256]{1,0:T(8,128)(2,1)}, bf16[7168,256]{1,0:T(8,128)(2,1)}, bf16[256,7168]{1,0:T(8,128)(2,1)}) custom-call(bf16[4,256,1792]{2,1,0:T(8,128)(2,1)S(1)} %bitcast.18, bf16[4,256,1792]{2,1,0:T(8,128)(2,1)S(1)} %bitcast.19, bf16[256,256]{1,0:T(8,128)(2,1)S(1)} %get-tuple-element.19.gg_ref, bf16[256,256]{1,0:T(8,128)(2,1)S(1)} %get-tuple-element.20.gu_ref, ...), custom_call_target="tpu_custom_call" | custom-call | flops 2818572288 | bytes 18350080 | tf_op jit(solution)/shard_map/wgrad/pallas_call | solution.py:387
  88.8 0.9 collective-permute-done
  89.7 0.8 copy.14
  90.5 0.6 copy.15
Async XLA Ops:
  0.6 1.1 %copy-start = (bf16[1,160,1792]{2,1,0:T(8,128)(2,1)S(1)}, bf16[1,160,1792]{2,1,0:T(8,128)(2,1)}, u32[]{:S(2)}) copy-start(bf16[1,160,1792]{2,1,0:T(8,128)(2,1)} %param.7) | copy-start | bytes 1720324
  1.7 0.7 copy-start.1
  2.4 0.7 copy-start.2
  74.0 15.7 %collective-permute-start = (bf16[1,160,1792]{2,1,0:T(8,128)(2,1)S(1)}, bf16[1,160,1792]{2,1,0:T(8,128)(2,1)S(1)}, u32[]{:S(2)}, u32[]{:S(2)}) collective-permute-start(bf16[1,160,1792]{2,1,0:T(8,128)(2,1)S(1)} %bitcast.20), channel_id=1, source_target_pairs={{0,24},{8,0},{16,8},{24,16},{1,25},{9,1},{17,9},{25,17},{2,26},{10... | collective-permute-start | bytes 1720328 | tf_op jit(solution)/shard_map/ppermute | solution.py:19
  77.7 2.0 %copy-start.3 = (bf16[4,2,128,1792]{3,2,1,0:T(8,128)(2,1)S(1)}, bf16[4,2,128,1792]{3,2,1,0:T(8,128)(2,1)}, u32[]{:S(2)}) copy-start(bf16[4,2,128,1792]{3,2,1,0:T(8,128)(2,1)} %get-tuple-element.17) | copy-start | bytes 11010052
  79.7 2.0 %copy-start.4 = (bf16[4,2,128,1792]{3,2,1,0:T(8,128)(2,1)S(1)}, bf16[4,2,128,1792]{3,2,1,0:T(8,128)(2,1)}, u32[]{:S(2)}) copy-start(bf16[4,2,128,1792]{3,2,1,0:T(8,128)(2,1)} %get-tuple-element.18) | copy-start | bytes 11010052

commit v2 on v1

--- a/solution.py
+++ b/solution.py
@@ -113,11 +113,11 @@
 
 def layer_kernel(
     T, K, C, F,
-    x_ref, dy_ref, routes_ref, gates_ref, wg_hbm, wu_hbm, wd_hbm,
-    ig_ref, gate_out_ref, gg_ref, gu_ref, ga_ref, rx_hbm, rd_hbm,
-    wg, wu, wd, pick, xf, rx, rd, xs, dys, gsend, grecv, pg, pu, hr,
-    sa, ra, sb, rb, own, sc, rc, gts, gtr,
-    send_sem, recv_sem, load_sem, out_sem,
+    x_hbm, dy_hbm, routes_ref, gates_ref, wg_hbm, wu_hbm, wd_hbm,
+    ig_ref, gate_out_ref, gw_ref, uw_ref, dw_ref,
+    pick, xf, dyv, rx, rd, xs, dys, gsend, grecv, pg, pu, hr, gg_ref, gu_ref, ga_ref,
+    sa, ra, sb, rb, own, sc, rc, fz, zr, gts, gtr,
+    send_sem, recv_sem, load_sem,
 ):
     n = lax.axis_index("node")
     l = lax.axis_index("local")
@@ -131,14 +131,17 @@
     c_mate = {"local": q_cm}
     y_mate = {"node": 1 - n}
 
+    z = lax.axis_index("section")
+    z_count = lax.axis_size("section")
+    x_load = pltpu.make_async_copy(x_hbm, xf.at[q_me], load_sem.at[3])
+    dy_load = pltpu.make_async_copy(dy_hbm, dyv, load_sem.at[4])
+    dy_load.start()
+    x_load.start()
     loads = [
-        pltpu.make_async_copy(wg_hbm, wg, load_sem.at[0]),
-        pltpu.make_async_copy(wu_hbm, wu, load_sem.at[1]),
+        pltpu.make_async_copy(wg_hbm, gw_ref, load_sem.at[0]),
+        pltpu.make_async_copy(wu_hbm, uw_ref, load_sem.at[1]),
+        pltpu.make_async_copy(wd_hbm, dw_ref, load_sem.at[2]),
     ]
-    for q in range(4):
-        loads.append(
-            pltpu.make_async_copy(wd_hbm.at[:, pl.ds(q * C, C)], wd.at[q], load_sem.at[2 + q])
-        )
 
     barrier = pltpu.get_barrier_semaphore()
     for dn in range(2):
@@ -148,7 +151,11 @@
                     barrier, inc=1, device_id_type=MESH,
                     device_id={"node": lax.rem(n + dn, 2), "local": lax.rem(l + dl, 4)},
                 )
-    pl.semaphore_wait(barrier, 7)
+    for dz in (1, z_count - 1):
+        pl.semaphore_signal(
+            barrier, inc=1, device_id_type=MESH, device_id={"section": lax.rem(z + dz, z_count)}
+        )
+    pl.semaphore_wait(barrier, 9)
 
     sent = []
 
@@ -161,7 +168,7 @@
         sent.append(d)
         return d
 
-    m0 = send(0, x_ref, xf.at[q_me], x_mate)
+    m0 = send(0, x_hbm, xf.at[q_me], x_mate)
 
     ids = routes_ref[...]
     before = lax.broadcasted_iota(jnp.int32, (T, T), 0) < lax.broadcasted_iota(jnp.int32, (T, T), 1)
@@ -181,19 +188,21 @@
     def select(g, rows):
         return jnp.dot(pick[g], rows, preferred_element_type=F32).astype(BF16)
 
-    dys[...] = select(1, dy_ref[...])
+    dy_load.wait()
+    dys[...] = select(1, dyv[...])
     m3 = send(3, dys, rd.at[q_me, 1], y_mate)
     gsend[...] = jnp.broadcast_to(columns[1], (K, 128)).astype(BF16)
     m14 = send(14, gsend, grecv, y_mate)
-    rd[q_me, 0] = select(0, dy_ref[...])
+    rd[q_me, 0] = select(0, dyv[...])
     m4 = send(4, rd.at[q_me, 0], rd.at[q_me, 0], x_mate)
-    xs[0] = select(1, x_ref[...])
+    x_load.wait()
+    xs[0] = select(1, xf[q_me])
     m10 = send(10, xs.at[0], rx.at[q_me, 1], y_mate)
     m5 = send(5, rd.at[q_me, 0], rd.at[q_me, 0], c_mate)
-    m1 = send(1, x_ref, xf.at[q_me], c_mate)
+    m1 = send(1, xf.at[q_me], xf.at[q_me], c_mate)
     for d in loads:
         d.start()
-    rx[q_me, 0] = select(0, x_ref[...])
+    rx[q_me, 0] = select(0, xf[q_me])
 
     m0.wait_recv()
     xs[1] = select(1, xf[q_xm])
@@ -220,12 +229,13 @@
 
     def project(q):
         rows = rx[q].reshape(2 * K, C)
-        pg[...] += jnp.dot(rows, wg[q], preferred_element_type=F32)
-        pu[...] += jnp.dot(rows, wu[q], preferred_element_type=F32)
+        pg[...] += jnp.dot(rows, gw_ref[q], preferred_element_type=F32)
+        pu[...] += jnp.dot(rows, uw_ref[q], preferred_element_type=F32)
 
     def hidden(q):
         rows = rd[q].reshape(2 * K, C)
-        hr[...] += lax.dot_general(rows, wd[q], NT, preferred_element_type=F32)
+        wide = pl.ds(pl.multiple_of(q * C, 256), C)
+        hr[...] += lax.dot_general(rows, dw_ref[:, wide], NT, preferred_element_type=F32)
 
     project(q_me)
     m12.wait_recv()
@@ -245,12 +255,6 @@
     hidden(q_cx)
     m13.wait_recv()
     project(q_cx)
-    out_copies = [
-        pltpu.make_async_copy(rx, rx_hbm, out_sem.at[0]),
-        pltpu.make_async_copy(rd, rd_hbm, out_sem.at[1]),
-    ]
-    for d in out_copies:
-        d.start()
     m14.wait_recv()
 
     parts = []
@@ -263,27 +267,27 @@
         gu_ref[rows] = d_up
         parts.append(part)
 
-    def terms(q, store):
-        @pl.loop(0, C // 256)
-        def _(j):
-            at = pl.ds(pl.multiple_of(j * 256, 256), 256)
-            t = lax.dot_general(gg_ref[...], wg[q, at], NT, preferred_element_type=F32)
-            t += lax.dot_general(gu_ref[...], wu[q, at], NT, preferred_element_type=F32)
-            t = t.astype(BF16)
-            for g in range(2):
-                store[g, :, at] = t[g * K : (g + 1) * K]
-
-    terms(q_cx, sa.at[0])
-    a0 = send(15, sa.at[0], ra.at[0], c_mate)
-    terms(q_xm, sb)
-    a0.wait_recv()
-    b = [None, None]
-    for g in (1, 0):
-        sb[g] = (sb[g].astype(F32) + ra[0, g].astype(F32)).astype(BF16)
-        b[g] = send(17 + g, sb.at[g], rb.at[g], x_mate)
-    terms(q_cm, sa.at[1])
-    a1 = send(16, sa.at[1], ra.at[1], c_mate)
-    terms(q_me, own)
+    def terms(q, j):
+        at = pl.ds(j * 256, 256)
+        t = lax.dot_general(gg_ref[...], gw_ref[q, at], NT, preferred_element_type=F32)
+        t += lax.dot_general(gu_ref[...], uw_ref[q, at], NT, preferred_element_type=F32)
+        return t.astype(BF16).reshape(2, K, 256)
+
+    chunks = C // 256
+    a0, a1, b, c, last = [], [], [], [], []
+
+    def across(j):
+        a0[j].wait_recv()
+        sb[j] = (sb[j].astype(F32) + ra[0, j].astype(F32)).astype(BF16)
+        b.append(send(15 + 2 * chunks + j, sb.at[j], rb.at[j], x_mate))
+
+    for j in range(chunks):
+        sa[0, j] = terms(q_cx, j)
+        a0.append(send(15 + j, sa.at[0, j], ra.at[0, j], c_mate))
+        sb[j] = terms(q_xm, j)
+        if j:
+            across(j - 1)
+    across(chunks - 1)
 
     eye = lax.broadcasted_iota(jnp.int32, (K, K), 0) == lax.broadcasted_iota(jnp.int32, (K, K), 1)
     for g in range(2):
@@ -292,17 +296,64 @@
         gts[g] = jnp.broadcast_to(row, (16, K)).astype(BF16)
     gtr[l] = gts[0]
     gate_sent = []
+    first = 15 + 5 * chunks
     for k in range(1, 4):
-        gate_sent.append(send(20 + k, gts.at[0], gtr.at[l], {"local": lax.rem(l + k, 4)}))
+        gate_sent.append(
+            send(first + k - 1, gts.at[0], gtr.at[l], {"local": lax.rem(l + k, 4)})
+        )
     for k in range(4):
         gate_sent.append(
-            send(24 + k, gts.at[1], gtr.at[4 + l], {"node": 1 - n, "local": lax.rem(l + k, 4)})
+            send(
+                first + 3 + k, gts.at[1], gtr.at[4 + l],
+                {"node": 1 - n, "local": lax.rem(l + k, 4)},
+            )
         )
 
-    a1.wait_recv()
-    b[1].wait_recv()
-    sc[...] = (own[1].astype(F32) + ra[1, 1].astype(F32) + rb[1].astype(F32)).astype(BF16)
-    c = send(19, sc, rc, y_mate)
+    for j in range(chunks):
+        sa[1, j] = terms(q_cm, j)
+        a1.append(send(15 + chunks + j, sa.at[1, j], ra.at[1, j], c_mate))
+        own[j] = terms(q_me, j)
+
+    def weights(j):
+        @pl.loop(0, 4)
+        def _(q):
+            at = pl.ds(j * 256, 256)
+            rows = rx[q, :, :, at].reshape(2 * K, 256)
+            grads = rd[q, :, :, at].reshape(2 * K, 256)
+            gw_ref[q, at] = lax.dot_general(
+                rows, gg_ref[...], TN, preferred_element_type=F32
+            ).astype(BF16)
+            uw_ref[q, at] = lax.dot_general(
+                rows, gu_ref[...], TN, preferred_element_type=F32
+            ).astype(BF16)
+            wide = pl.ds(pl.multiple_of(q * C + j * 256, 256), 256)
+            dw_ref[:, wide] = lax.dot_general(
+                ga_ref[...], grads, TN, preferred_element_type=F32
+            ).astype(BF16)
+
+    def finish(j):
+        c[j].wait_recv()
+        t = lax.dot_general(pick[0], own[j, 0], TN, preferred_element_type=F32)
+        t += lax.dot_general(pick[1], rc[j], TN, preferred_element_type=F32)
+        fz[j] = t.astype(BF16)
+        last.append(
+            send(
+                15 + 4 * chunks + j, fz.at[j], zr.at[j],
+                {"section": lax.rem(z + z_count - 1, z_count)},
+            )
+        )
+
+    for j in range(chunks):
+        a1[j].wait_recv()
+        b[j].wait_recv()
+        whole = own[j].astype(F32) + ra[1, j].astype(F32) + rb[j].astype(F32)
+        whole = whole.astype(BF16)
+        sc[j] = whole[1]
+        c.append(send(15 + 3 * chunks + j, sc.at[j], rc.at[j], y_mate))
+        own[j, 0] = whole[0]
+        if j:
+            finish(j - 1)
+        weights(j)
     for d in gate_sent:
         d.wait_recv()
     total = jnp.zeros((16, T), F32)
@@ -312,31 +363,25 @@
             row += gtr[4 * g + k].astype(F32)
         total += jnp.dot(row.astype(BF16), pick[g], preferred_element_type=F32)
     gate_out_ref[...] = total[0:1]
-
-    b[0].wait_recv()
-    own[0] = (own[0].astype(F32) + ra[1, 0].astype(F32) + rb[0].astype(F32)).astype(BF16)
-    c.wait_recv()
-
-    @pl.loop(0, C // 256)
-    def _(j):
-        at = pl.ds(pl.multiple_of(j * 256, 256), 256)
-        t = lax.dot_general(pick[0], own[0, :, at], TN, preferred_element_type=F32)
-        t += lax.dot_general(pick[1], rc[:, at], TN, preferred_element_type=F32)
-        ig_ref[:, at] = t.astype(BF16)
-
+    finish(chunks - 1)
+    for j in range(chunks):
+        last[j].wait_recv()
+        ig_ref[:, j * 256 : (j + 1) * 256] = zr[j]
     for d in sent:
         d.wait_send()
-    for d in out_copies:
+
+
+def store_kernel(gw_ref, uw_ref, dw_ref, gw_out, uw_out, dw_out, sem):
+    copies = []
+    for k, (src, dst) in enumerate(((gw_ref, gw_out), (uw_ref, uw_out), (dw_ref, dw_out))):
+        part = src.shape[0] // 4
+        for i in range(4):
+            at = pl.ds(i * part, part)
+            copies.append(pltpu.make_async_copy(src.at[at], dst.at[at], sem.at[4 * k + i]))
+    for d in copies:
+        d.start()
+    for d in copies:
         d.wait()
-
-
-def wgrad_kernel(rx_ref, rd_ref, gg_ref, gu_ref, ga_ref, gw_ref, uw_ref, dw_ref):
-    rows = rx_ref[0]
-    gw_ref[...] = lax.dot_general(rows, gg_ref[...], TN, preferred_element_type=F32).astype(BF16)
-    uw_ref[...] = lax.dot_general(rows, gu_ref[...], TN, preferred_element_type=F32).astype(BF16)
-    dw_ref[...] = lax.dot_general(
-        ga_ref[...], rd_ref[0], TN, preferred_element_type=F32
-    ).astype(BF16)
 
 
 def fused_body(layer_input, out_grad, routes, gates, gate_weight, up_weight, down_weight):
@@ -347,57 +392,52 @@
     hbm = pl.BlockSpec(memory_space=pl.ANY)
     shape = jax.ShapeDtypeStruct
     rows = (4, 2, K, C)
-    ig, gate_grad, gg, gu, ga, rx, rd = pl.pallas_call(
+    chunk = (C // 256, K, 256)
+    pair = (C // 256, 2, K, 256)
+    last = (C // 256, T, 256)
+    ig, gate_grad, gw, uw, dw = pl.pallas_call(
         functools.partial(layer_kernel, T, K, C, F),
         out_shape=(
             shape((T, C), BF16), shape((1, T), F32),
-            shape((2 * K, F), BF16), shape((2 * K, F), BF16), shape((2 * K, F), BF16),
-            shape(rows, BF16), shape(rows, BF16),
+            shape((4, C, F), BF16), shape((4, C, F), BF16), shape((F, D), BF16),
         ),
-        in_specs=[vmem] * 4 + [hbm] * 3,
-        out_specs=(vmem,) * 5 + (hbm,) * 2,
+        in_specs=[hbm] * 2 + [vmem] * 2 + [hbm] * 3,
+        out_specs=(vmem,) * 5,
         scratch_shapes=[
-            pltpu.VMEM((4, C, F), BF16), pltpu.VMEM((4, C, F), BF16), pltpu.VMEM((4, F, C), BF16),
-            pltpu.VMEM((2, K, T), BF16), pltpu.VMEM((4, T, C), BF16),
+            pltpu.VMEM((2, K, T), BF16), pltpu.VMEM((4, T, C), BF16), pltpu.VMEM((T, C), BF16),
             pltpu.VMEM(rows, BF16), pltpu.VMEM(rows, BF16),
             pltpu.VMEM((2, K, C), BF16), pltpu.VMEM((K, C), BF16),
             pltpu.VMEM((K, 128), BF16), pltpu.VMEM((K, 128), BF16),
             pltpu.VMEM((2 * K, F), F32), pltpu.VMEM((2 * K, F), F32), pltpu.VMEM((2 * K, F), F32),
-            pltpu.VMEM((2, 2, K, C), BF16), pltpu.VMEM((2, 2, K, C), BF16),
-            pltpu.VMEM((2, K, C), BF16), pltpu.VMEM((2, K, C), BF16), pltpu.VMEM((2, K, C), BF16),
-            pltpu.VMEM((K, C), BF16), pltpu.VMEM((K, C), BF16),
+            pltpu.VMEM((2 * K, F), BF16), pltpu.VMEM((2 * K, F), BF16), pltpu.VMEM((2 * K, F), BF16),
+            pltpu.VMEM((2,) + pair, BF16), pltpu.VMEM((2,) + pair, BF16),
+            pltpu.VMEM(pair, BF16), pltpu.VMEM(pair, BF16), pltpu.VMEM(pair, BF16),
+            pltpu.VMEM(chunk, BF16), pltpu.VMEM(chunk, BF16),
+            pltpu.VMEM(last, BF16), pltpu.VMEM(last, BF16),
             pltpu.VMEM((2, 16, K), BF16), pltpu.VMEM((8, 16, K), BF16),
-            pltpu.SemaphoreType.DMA((28,)), pltpu.SemaphoreType.DMA((28,)),
-            pltpu.SemaphoreType.DMA((6,)), pltpu.SemaphoreType.DMA((2,)),
+            pltpu.SemaphoreType.DMA((22 + 5 * (C // 256),)),
+            pltpu.SemaphoreType.DMA((22 + 5 * (C // 256),)),
+            pltpu.SemaphoreType.DMA((5,)),
         ],
         compiler_params=pltpu.CompilerParams(
-            collective_id=0, has_side_effects=True, vmem_limit_bytes=52 * 2**20
+            collective_id=0, has_side_effects=True, vmem_limit_bytes=41 * 2**20
         ),
         name="layer",
     )(
         layer_input[0], out_grad[0], routes.reshape(1, T), gates.reshape(1, T),
         gate_weight.reshape(4, C, F), up_weight.reshape(4, C, F), down_weight.reshape(F, D),
     )
-    passed = from_behind(ig[None], "section", -1)
-    half = C // 2
-    slab = pl.BlockSpec((1, 2 * K, half), lambda i: (i // 2, 0, i % 2))
-    units = pl.BlockSpec((2 * K, F), lambda i: (0, 0))
-    tall = pl.BlockSpec((half, F), lambda i: (i, 0))
-    wide = pl.BlockSpec((F, half), lambda i: (0, i))
     gw, uw, dw = pl.pallas_call(
-        wgrad_kernel,
-        grid=(8,),
+        store_kernel,
         out_shape=(shape((D, F), BF16), shape((D, F), BF16), shape((F, D), BF16)),
-        in_specs=[slab, slab, units, units, units],
-        out_specs=(tall, tall, wide),
-        compiler_params=pltpu.CompilerParams(vmem_limit_bytes=24 * 2**20),
-        cost_estimate=pl.CostEstimate(
-            flops=12 * K * D * F, bytes_accessed=8 * K * D + 6 * D * F, transcendentals=0
-        ),
-        name="wgrad",
-    )(rx.reshape(4, 2 * K, C), rd.reshape(4, 2 * K, C), gg, gu, ga)
+        in_specs=[vmem] * 3,
+        out_specs=(hbm,) * 3,
+        scratch_shapes=[pltpu.SemaphoreType.DMA((12,))],
+        compiler_params=pltpu.CompilerParams(vmem_limit_bytes=16 * 2**20),
+        name="store",
+    )(gw.reshape(D, F), uw.reshape(D, F), dw)
     return (
-        passed, gate_grad.reshape(1, T, 1), gw[None, None], uw[None, None], dw[None, None]
+        ig[None], gate_grad.reshape(1, T, 1), gw[None, None], uw[None, None], dw[None, None]
     )
 
 

time: 91.4 us -> 82.7 us (0.905)
  starting transfers between devices: 3.67 us -> 0 us
  local copies, waits for them, and re-layouts: 7.86 us -> 4.84 us
  Pallas kernels: 78 us -> 76.9 us
    ppermute x1 -> x0, starting transfers between devices: 3.67 us -> none  [from_behind(): lax.ppermute(value, axis, [(i, (i + by) % length) for i in range(length)])]
    unnamed x12 -> x10, local copies, waits for them, and re-layouts: 7.86 us -> 4.84 us
    pallas_call x1, Pallas kernels: 7.03 us -> 4.2 us  [fused_body(): pl.pallas_call(store_kernel, out_shape=(shape((D, F), BF16), shape((D, F)...]
    pallas_call x1, Pallas kernels: 70.9 us -> 72.7 us  [fused_body(): pl.pallas_call(functools.partial(layer_kernel, T, K, C, F), out_shape=(sh...]
  transfers between devices with their start and end apart: 1 -> 0, of which waited for: 1 -> 0; matrix products, arithmetic and copies ran while one was open for 0% -> 0% of each run, Pallas kernels for 8% -> 0%
where the time goes in v2:
time: 82.7 us; the launch traced here: 82.4 us
  Pallas kernels  76.9 us (93%)
  local copies, waits for them, and re-layouts  4.84 us (6%)
    pallas_call x1, Pallas kernels, fused_body(): pl.pallas_call(functools.partial(layer_kernel, T, K, C, F), out_shape=(sh...  72.7 us
    unnamed x10, local copies, waits for them, and re-layouts  4.84 us
    pallas_call x1, Pallas kernels, fused_body(): pl.pallas_call(store_kernel, out_shape=(shape((D, F), BF16), shape((D, F)...  4.2 us

profile of v2, /device:TPU:0, one launch (start us, length us, event | category | flops | bytes accessed | tf_op | source)
XLA Modules:
  0.0 82.4 jit_solution(12309992712400669814)
XLA Ops:
  0.6 0.0 copy-start
  0.6 1.1 %copy-done = bf16[1,160,1792]{2,1,0:T(8,128)(2,1)S(1)} copy-done((bf16[1,160,1792]{2,1,0:T(8,128)(2,1)S(1)}, bf16[1,160,1792]{2,1,0:T(8,128)(2,1)}, u32[]{:S(2)}) %copy-start) | copy-done | bytes 573464
  1.7 0.0 copy-start.1
  1.7 1.1 %copy-done.1 = bf16[1,160,1792]{2,1,0:T(8,128)(2,1)S(1)} copy-done((bf16[1,160,1792]{2,1,0:T(8,128)(2,1)S(1)}, bf16[1,160,1792]{2,1,0:T(8,128)(2,1)}, u32[]{:S(2)}) %copy-start.1) | copy-done | bytes 573464
  2.8 0.0 copy-start.2
  2.8 0.7 copy-done.2
  3.4 0.0 copy-start.3
  3.4 0.7 copy-done.3
  4.1 72.7 %layer.1 = (bf16[160,1792]{1,0:T(8,128)(2,1)S(1)}, f32[1,160]{1,0:T(1,128)S(1)}, bf16[4,1792,256]{2,1,0:T(8,128)(2,1)S(1)}, bf16[4,1792,256]{2,1,0:T(8,128)(2,1)S(1)}, bf16[256,7168]{1,0:T(8,128)(2,1)S(1)}) custom-call(bf16[160,1792]{1,0:T(8,128)(2,1)S(1)} %bitcast.16, bf16[160,1792]{1,0:T(8,128)(2,1)S(1)} %bitcast.17, s32[1,160]{1,0:T(1,128)S(1)} %bitcast.19, ...), custom_call_target="tpu_custom_call" | custom-call | tf_op jit(solution)/shard_map/layer/pallas_call | solution.py:398
  76.9 4.2 %store.1 = (bf16[7168,256]{1,0:T(8,128)(2,1)}, bf16[7168,256]{1,0:T(8,128)(2,1)}, bf16[256,7168]{1,0:T(8,128)(2,1)}) custom-call(bf16[7168,256]{1,0:T(8,128)(2,1)S(1)} %bitcast.14, bf16[7168,256]{1,0:T(8,128)(2,1)S(1)} %bitcast.15, bf16[256,7168]{1,0:T(8,128)(2,1)S(1)} %get-tuple-element.17.dw_ref), custom_call_target="tpu_custom_call" | custom-call | tf_op jit(solution)/shard_map/store/pallas_call | solution.py:430
  81.1 0.8 copy.14
  81.9 0.6 copy.15
Async XLA Ops:
  0.6 1.1 %copy-start = (bf16[1,160,1792]{2,1,0:T(8,128)(2,1)S(1)}, bf16[1,160,1792]{2,1,0:T(8,128)(2,1)}, u32[]{:S(2)}) copy-start(bf16[1,160,1792]{2,1,0:T(8,128)(2,1)} %param.7) | copy-start | bytes 1720324
  1.7 1.1 %copy-start.1 = (bf16[1,160,1792]{2,1,0:T(8,128)(2,1)S(1)}, bf16[1,160,1792]{2,1,0:T(8,128)(2,1)}, u32[]{:S(2)}) copy-start(bf16[1,160,1792]{2,1,0:T(8,128)(2,1)} %param.8) | copy-start | bytes 1720324
  2.8 0.7 copy-start.2
  3.4 0.7 copy-start.3

commit v3 on v2

--- a/solution.py
+++ b/solution.py
@@ -113,9 +113,9 @@
 
 def layer_kernel(
     T, K, C, F,
-    x_hbm, dy_hbm, routes_ref, gates_ref, wg_hbm, wu_hbm, wd_hbm,
+    x_hbm, dy_hbm, routes_hbm, gates_ref, wg_hbm, wu_hbm, wd_hbm,
     ig_ref, gate_out_ref, gw_ref, uw_ref, dw_ref,
-    pick, xf, dyv, rx, rd, xs, dys, gsend, grecv, pg, pu, hr, gg_ref, gu_ref, ga_ref,
+    routes_ref, pick, xf, dyv, rx, rd, xs, dys, gsend, grecv, pg, pu, hr, gg_ref, gu_ref, ga_ref,
     sa, ra, sb, rb, own, sc, rc, fz, zr, gts, gtr,
     send_sem, recv_sem, load_sem,
 ):
@@ -135,6 +135,8 @@
     z_count = lax.axis_size("section")
     x_load = pltpu.make_async_copy(x_hbm, xf.at[q_me], load_sem.at[3])
     dy_load = pltpu.make_async_copy(dy_hbm, dyv, load_sem.at[4])
+    routes_load = pltpu.make_async_copy(routes_hbm, routes_ref, load_sem.at[5])
+    routes_load.start()
     dy_load.start()
     x_load.start()
     loads = [
@@ -170,6 +172,7 @@
 
     m0 = send(0, x_hbm, xf.at[q_me], x_mate)
 
+    routes_load.wait()
     ids = routes_ref[...]
     before = lax.broadcasted_iota(jnp.int32, (T, T), 0) < lax.broadcasted_iota(jnp.int32, (T, T), 1)
     before = jnp.where(before, 1.0, 0.0).astype(BF16)
@@ -371,13 +374,15 @@
         d.wait_send()
 
 
-def store_kernel(gw_ref, uw_ref, dw_ref, gw_out, uw_out, dw_out, sem):
+def store_kernel(ig_ref, gate_ref, gw_ref, uw_ref, dw_ref, ig_out, gate_out, gw_out, uw_out, dw_out, sem):
     copies = []
     for k, (src, dst) in enumerate(((gw_ref, gw_out), (uw_ref, uw_out), (dw_ref, dw_out))):
         part = src.shape[0] // 4
         for i in range(4):
             at = pl.ds(i * part, part)
             copies.append(pltpu.make_async_copy(src.at[at], dst.at[at], sem.at[4 * k + i]))
+    copies.append(pltpu.make_async_copy(ig_ref, ig_out, sem.at[12]))
+    copies.append(pltpu.make_async_copy(gate_ref, gate_out, sem.at[13]))
     for d in copies:
         d.start()
     for d in copies:
@@ -390,6 +395,7 @@
     K = -(-(3 * T // 4) // 128) * 128
     vmem = pl.BlockSpec(memory_space=pltpu.VMEM)
     hbm = pl.BlockSpec(memory_space=pl.ANY)
+    far = pl.BlockSpec(memory_space=pltpu.HBM)
     shape = jax.ShapeDtypeStruct
     rows = (4, 2, K, C)
     chunk = (C // 256, K, 256)
@@ -401,10 +407,10 @@
             shape((T, C), BF16), shape((1, T), F32),
             shape((4, C, F), BF16), shape((4, C, F), BF16), shape((F, D), BF16),
         ),
-        in_specs=[hbm] * 2 + [vmem] * 2 + [hbm] * 3,
+        in_specs=[far] * 3 + [vmem] + [far] * 3,
         out_specs=(vmem,) * 5,
         scratch_shapes=[
-            pltpu.VMEM((2, K, T), BF16), pltpu.VMEM((4, T, C), BF16), pltpu.VMEM((T, C), BF16),
+            pltpu.VMEM((1, T), jnp.int32), pltpu.VMEM((2, K, T), BF16), pltpu.VMEM((4, T, C), BF16), pltpu.VMEM((T, C), BF16),
             pltpu.VMEM(rows, BF16), pltpu.VMEM(rows, BF16),
             pltpu.VMEM((2, K, C), BF16), pltpu.VMEM((K, C), BF16),
             pltpu.VMEM((K, 128), BF16), pltpu.VMEM((K, 128), BF16),
@@ -417,7 +423,7 @@
             pltpu.VMEM((2, 16, K), BF16), pltpu.VMEM((8, 16, K), BF16),
             pltpu.SemaphoreType.DMA((22 + 5 * (C // 256),)),
             pltpu.SemaphoreType.DMA((22 + 5 * (C // 256),)),
-            pltpu.SemaphoreType.DMA((5,)),
+            pltpu.SemaphoreType.DMA((6,)),
         ],
         compiler_params=pltpu.CompilerParams(
             collective_id=0, has_side_effects=True, vmem_limit_bytes=41 * 2**20
@@ -427,15 +433,15 @@
         layer_input[0], out_grad[0], routes.reshape(1, T), gates.reshape(1, T),
         gate_weight.reshape(4, C, F), up_weight.reshape(4, C, F), down_weight.reshape(F, D),
     )
-    gw, uw, dw = pl.pallas_call(
+    ig, gate_grad, gw, uw, dw = pl.pallas_call(
         store_kernel,
-        out_shape=(shape((D, F), BF16), shape((D, F), BF16), shape((F, D), BF16)),
-        in_specs=[vmem] * 3,
-        out_specs=(hbm,) * 3,
-        scratch_shapes=[pltpu.SemaphoreType.DMA((12,))],
+        out_shape=(shape((T, C), BF16), shape((1, T), F32), shape((D, F), BF16), shape((D, F), BF16), shape((F, D), BF16)),
+        in_specs=[vmem] * 5,
+        out_specs=(far,) * 5,
+        scratch_shapes=[pltpu.SemaphoreType.DMA((14,))],
         compiler_params=pltpu.CompilerParams(vmem_limit_bytes=16 * 2**20),
         name="store",
-    )(gw.reshape(D, F), uw.reshape(D, F), dw)
+    )(ig, gate_grad, gw.reshape(D, F), uw.reshape(D, F), dw)
     return (
         ig[None], gate_grad.reshape(1, T, 1), gw[None, None], uw[None, None], dw[None, None]
     )

time: 82.7 us -> 81.5 us (0.985)
  local copies, waits for them, and re-layouts: 4.84 us -> 3.47 us
    unnamed x10 -> x8, local copies, waits for them, and re-layouts: 4.84 us -> 3.47 us
where the time goes in v3:
time: 81.5 us; the launch traced here: 81.2 us
  Pallas kernels  77.1 us (95%)
  local copies, waits for them, and re-layouts  3.47 us (4%)
    pallas_call x1, Pallas kernels, fused_body(): pl.pallas_call(functools.partial(layer_kernel, T, K, C, F), out_shape=(sh...  72.7 us
    pallas_call x1, Pallas kernels, fused_body(): pl.pallas_call(store_kernel, out_shape=(shape((T, C), BF16), shape((1, T)...  4.38 us
    unnamed x8, local copies, waits for them, and re-layouts  3.47 us

profile of v3, /device:TPU:0, one launch (start us, length us, event | category | flops | bytes accessed | tf_op | source)
XLA Modules:
  0.0 81.2 jit_solution(9632412664550109635)
XLA Ops:
  0.6 0.0 copy-start
  0.6 1.1 %copy-done = bf16[1,160,1792]{2,1,0:T(8,128)(2,1)S(1)} copy-done((bf16[1,160,1792]{2,1,0:T(8,128)(2,1)S(1)}, bf16[1,160,1792]{2,1,0:T(8,128)(2,1)}, u32[]{:S(2)}) %copy-start) | copy-done | bytes 573464
  1.7 0.0 copy-start.1
  1.7 1.1 %copy-done.1 = bf16[1,160,1792]{2,1,0:T(8,128)(2,1)S(1)} copy-done((bf16[1,160,1792]{2,1,0:T(8,128)(2,1)S(1)}, bf16[1,160,1792]{2,1,0:T(8,128)(2,1)}, u32[]{:S(2)}) %copy-start.1) | copy-done | bytes 573464
  2.8 0.0 copy-start.2
  2.8 0.7 copy-done.2
  3.4 0.0 copy-start.3
  3.4 0.7 copy-done.3
  4.1 72.7 %layer.1 = (bf16[160,1792]{1,0:T(8,128)(2,1)S(1)}, f32[1,160]{1,0:T(1,128)S(1)}, bf16[4,1792,256]{2,1,0:T(8,128)(2,1)S(1)}, bf16[4,1792,256]{2,1,0:T(8,128)(2,1)S(1)}, bf16[256,7168]{1,0:T(8,128)(2,1)S(1)}) custom-call(bf16[160,1792]{1,0:T(8,128)(2,1)S(1)} %bitcast.16, bf16[160,1792]{1,0:T(8,128)(2,1)S(1)} %bitcast.17, s32[1,160]{1,0:T(1,128)S(1)} %bitcast.18, ...), custom_call_target="tpu_custom_call" | custom-call | tf_op jit(solution)/shard_map/layer/pallas_call | solution.py:404
  76.9 4.4 %store.1 = (bf16[160,1792]{1,0:T(8,128)(2,1)}, f32[1,160]{1,0:T(1,128)}, bf16[7168,256]{1,0:T(8,128)(2,1)}, bf16[7168,256]{1,0:T(8,128)(2,1)}, bf16[256,7168]{1,0:T(8,128)(2,1)}) custom-call(bf16[160,1792]{1,0:T(8,128)(2,1)S(1)} %get-tuple-element.15.ig_ref, f32[1,160]{1,0:T(1,128)S(1)} %get-tuple-element.16.gate_ref, bf16[7168,256]{1,0:T(8,128)(2,1)S(1)} %bitcast.14, ...), custom_call_target="tpu_custom_call" | custom-call | tf_op jit(solution)/shard_map/store/pallas_call | solution.py:436
Async XLA Ops:
  0.6 1.1 %copy-start = (bf16[1,160,1792]{2,1,0:T(8,128)(2,1)S(1)}, bf16[1,160,1792]{2,1,0:T(8,128)(2,1)}, u32[]{:S(2)}) copy-start(bf16[1,160,1792]{2,1,0:T(8,128)(2,1)} %param.7) | copy-start | bytes 1720324
  1.7 1.1 %copy-start.1 = (bf16[1,160,1792]{2,1,0:T(8,128)(2,1)S(1)}, bf16[1,160,1792]{2,1,0:T(8,128)(2,1)}, u32[]{:S(2)}) copy-start(bf16[1,160,1792]{2,1,0:T(8,128)(2,1)} %param.8) | copy-start | bytes 1720324
  2.8 0.7 copy-start.2
  3.4 0.7 copy-start.3
